TPU v7x, 512 devices: a whole 4x4x16 slice. The times are simulated.
512 devices in a mesh: leaf: 64 (over z, y), front: 8 (over x, core).
Axes of the slice: x: 4, y: 4, z: 16, core: 2. Of those that a mesh axis runs over, the one named last changes fastest.
Arguments:
- top_factor: float32 [1408, 2816], P('front', 'leaf'), may hold values from -1 to 3
- panel_two: float32 [1408, 5632], P('front', 'leaf'), may hold values from -0.109375 to 0.109375
- panel_three: float32 [1408, 11264], P('front', 'leaf'), may hold values from -0.109375 to 0.109375
- panel_four: float32 [1408, 22528], P('front', 'leaf'), may hold values from -0.109375 to 0.109375
- factor_two: float32 [1408, 5632], P('front', 'leaf'), may hold values from -1 to 3
- factor_three: float32 [1408, 11264], P('front', 'leaf'), may hold values from -1 to 3
- factor_four: float32 [1408, 22528], P('front', 'leaf'), may hold values from -1 to 3
Outputs:
- cov_one: float32 [1408, 2816], P('front', 'leaf')
- cross_two: float32 [1408, 5632], P('front', 'leaf')
- cov_two: float32 [1408, 5632], P('front', 'leaf')
- cross_three: float32 [1408, 11264], P('front', 'leaf')
- cov_three: float32 [1408, 11264], P('front', 'leaf')
- cross_four: float32 [1408, 22528], P('front', 'leaf')
- cov_four: float32 [1408, 22528], P('front', 'leaf')
All inputs are finite; a program needn't handle non-finite values.
Results may differ from a plain program's by a relative error of at most 0.000088.
Values sent between devices are 32-bit elements; how exact they have to be, the bound alone decides.
No kernel may reach another device: no remote copies, remote signals or barrier semaphores. Data moves between devices by JAX's collectives and lax.ppermute only.
A program may use at most 64 MiB of HBM per device.

v0:
```python
import jax
import jax.numpy as jnp
from jax import lax
from jax.sharding import PartitionSpec as P

S = 1408


def from_partner(value, axis, distance):
    mask = 2**distance
    pairs = [(source, source ^ mask) for source in range(lax.axis_size(axis))]
    return lax.ppermute(value, axis, pairs)


def product(first, second):
    return jnp.dot(
        first, second, precision=lax.Precision.HIGHEST, preferred_element_type=jnp.float32
    )


def inner_product(first, second):
    return lax.dot_general(
        first,
        second,
        (((0,), (0,)), ((), ())),
        precision=lax.Precision.HIGHEST,
        preferred_element_type=jnp.float32,
    )


def cube_rows(block_tile, cube_size):
    position = lax.axis_index("leaf")
    joined = block_tile
    for bit_index in range(cube_size.bit_length() - 1):
        partner = from_partner(joined, "leaf", bit_index)
        is_upper = jnp.right_shift(position, bit_index) % 2 == 1
        joined = jnp.where(
            is_upper, jnp.concatenate([partner, joined], -1), jnp.concatenate([joined, partner], -1)
        )
    return joined


def local(top_factor, panel_two, panel_three, panel_four, factor_two, factor_three, factor_four):
    share_rows = S // lax.axis_size("front")

    def front_sum(term_fn):
        return lax.psum_scatter(
            term_fn(jnp.int32(0), share_rows * lax.axis_size("front")),
            "front",
            scatter_dimension=0,
            tiled=True,
        )

    top_rows = cube_rows(top_factor, S // top_factor.shape[1])

    def top_term(offset, amount):
        return inner_product(top_rows, top_factor)

    parent = front_sum(top_term)
    results = [parent]
    for panel_tile, factor_tile in (
        (panel_two, factor_two),
        (panel_three, factor_three),
        (panel_four, factor_four),
    ):
        tile_width = panel_tile.shape[1]
        cube_size = S // tile_width
        parent_rows = cube_rows(parent, S // parent.shape[1])
        cross_block = -product(parent_rows, lax.all_gather(panel_tile, "front", axis=0, tiled=True))
        stacked = cube_rows(jnp.stack([cross_block, factor_tile]), cube_size)

        def level_term(offset, amount):
            gram_part = inner_product(stacked[1], factor_tile)
            return gram_part - inner_product(stacked[0], panel_tile)

        covariance = front_sum(level_term)
        results.append(cross_block)
        results.append(covariance)
        parent = covariance
    return tuple(results)


def solution(mesh):
    return jax.shard_map(
        local,
        mesh=mesh,
        in_specs=(
            P("front", "leaf"),
            P("front", "leaf"),
            P("front", "leaf"),
            P("front", "leaf"),
            P("front", "leaf"),
            P("front", "leaf"),
            P("front", "leaf"),
        ),
        out_specs=(
            P("front", "leaf"),
            P("front", "leaf"),
            P("front", "leaf"),
            P("front", "leaf"),
            P("front", "leaf"),
            P("front", "leaf"),
            P("front", "leaf"),
        ),
        check_vma=False,
    )
```

profile of v0, /device:TPU:8, one launch (start us, length us, event | category | flops | bytes accessed | tf_op | source)
XLA Modules:
  0.0 660.0 jit_solution(10126110818156442605)
XLA Ops:
  8.1 7.7 %collective-permute-start = (f32[176,44]{1,0:T(8,128)S(1)}, f32[176,44]{1,0:T(8,128)S(1)}, u32[]{:S(2)}, u32[]{:S(2)}) collective-permute-start(f32[176,44]{1,0:T(8,128)S(1)} %copy.16), channel_id=1, source_target_pairs={{0,8},{8,0},{16,24},{24,16},{32,40},{40,32},{48,56},{56,48},{64,72... | collective-permute-start | bytes 92936 | tf_op jit(solution)/shard_map/ppermute | solution.py:12
  15.9 2.5 collective-permute-done
  18.5 1.9 collective-permute-start.1
  20.4 6.0 collective-permute-done.1
  26.6 1.9 collective-permute-start.2
  28.5 6.7 %collective-permute-done.2 = f32[176,176]{1,0:T(8,128)S(1)} collective-permute-done((f32[176,176]{1,0:T(8,128)S(1)}, f32[176,176]{1,0:T(8,128)S(1)}, u32[]{:S(2)}, u32[]{:S(2)}) %collective-permute-start.2) | collective-permute-done | bytes 123936 | tf_op jit(solution)/shard_map/ppermute | solution.py:12
  35.4 1.9 collective-permute-start.3
  37.3 9.2 %collective-permute-done.3 = f32[176,352]{1,0:T(8,128)S(1)} collective-permute-done((f32[176,352]{1,0:T(8,128)S(1)}, f32[176,352]{1,0:T(8,128)S(1)}, u32[]{:S(2)}, u32[]{:S(2)}) %collective-permute-start.3) | collective-permute-done | bytes 247840 | tf_op jit(solution)/shard_map/ppermute | solution.py:12
  46.8 7.1 %collective-permute-start.4 = (f32[176,704]{1,0:T(8,128)S(1)}, f32[176,704]{1,0:T(8,128)S(1)}, u32[]{:S(2)}, u32[]{:S(2)}) collective-permute-start(f32[176,704]{1,0:T(8,128)S(1)} %maximum_select_fusion.15), channel_id=1, source_target_pairs={{0,128},{8,136},{16,144},{24,152},{32,160},{40,168},{48,176},{56,1... | collective-permute-start | bytes 1486856 | tf_op jit(solution)/shard_map/ppermute | solution.py:12
  53.9 44.9 %collective-permute-done.4 = f32[176,704]{1,0:T(8,128)S(1)} collective-permute-done((f32[176,704]{1,0:T(8,128)S(1)}, f32[176,704]{1,0:T(8,128)S(1)}, u32[]{:S(2)}, u32[]{:S(2)}) %collective-permute-start.4) | collective-permute-done | bytes 495648 | tf_op jit(solution)/shard_map/ppermute | solution.py:12
  98.8 3.6 fusion.3
  102.5 40.2 %reduce-scatter.13.cloned.1.call-done = f32[176,44]{1,0:T(8,128)} async-done(((f32[1408,44]{1,0:T(8,128)}), f32[176,44]{1,0:T(8,128)}) %reduce-scatter.13.cloned.1.call-update) | async-done | bytes 30992 | tf_op jit(solution)/shard_map/reduce_scatter | solution.py:47
  142.7 2.4 collective-permute-start.5
  145.2 4.2 collective-permute-done.5
  150.5 4.0 collective-permute-start.6
  154.5 3.9 collective-permute-done.6
  158.6 3.4 collective-permute-start.7
  162.0 5.5 collective-permute-done.7
  167.7 4.4 collective-permute-start.8
  172.2 7.6 %collective-permute-done.8 = f32[176,352]{1,0:T(8,128)S(1)} collective-permute-done((f32[176,352]{1,0:T(8,128)S(1)}, f32[176,352]{1,0:T(8,128)S(1)}, u32[]{:S(2)}, u32[]{:S(2)}) %collective-permute-start.8) | collective-permute-done | bytes 247840 | tf_op jit(solution)/shard_map/ppermute | solution.py:12
  180.0 22.2 %collective-permute-start.9 = (f32[176,704]{1,0:T(8,128)S(1)}, f32[176,704]{1,0:T(8,128)S(1)}, u32[]{:S(2)}, u32[]{:S(2)}) collective-permute-start(f32[176,704]{1,0:T(8,128)S(1)} %maximum_select_fusion.16), channel_id=1, source_target_pairs={{0,128},{8,136},{16,144},{24,152},{32,160},{40,168},{48,176},{56,1... | collective-permute-start | bytes 1486856 | tf_op jit(solution)/shard_map/ppermute | solution.py:12
  202.4 13.3 %all_gather.9 = f32[1408,88]{1,0:T(8,128)S(1)} all-gather(f32[176,88]{1,0:T(8,128)S(1)} %copy-done.6), channel_id=1, replica_groups=mesh['leaf'=64,'front'=8] {'front'}, dimensions={0}, use_global_device_ids=true | all-gather | bytes 557568 | tf_op jit(solution)/shard_map/all_gather | solution.py:69
  215.7 10.3 %collective-permute-done.9 = f32[176,704]{1,0:T(8,128)S(1)} collective-permute-done((f32[176,704]{1,0:T(8,128)S(1)}, f32[176,704]{1,0:T(8,128)S(1)}, u32[]{:S(2)}, u32[]{:S(2)}) %collective-permute-start.9) | collective-permute-done | bytes 495648 | tf_op jit(solution)/shard_map/ppermute | solution.py:12
  227.7 2.9 collective-permute-start.10
  230.6 4.5 collective-permute-done.10
  235.1 4.0 collective-permute-start.11
  239.2 6.8 %collective-permute-done.11 = f32[2,176,176]{1,2,0:T(8,128)S(1)} collective-permute-done((f32[2,176,176]{1,2,0:T(8,128)S(1)}, f32[2,176,176]{1,2,0:T(8,128)S(1)}, u32[]{:S(2)}, u32[]{:S(2)}) %collective-permute-start.11) | collective-permute-done | bytes 247840 | tf_op jit(solution)/shard_map/ppermute | solution.py:12
  246.3 1.9 collective-permute-start.12
  248.2 9.3 %collective-permute-done.12 = f32[2,176,352]{2,1,0:T(8,128)S(1)} collective-permute-done((f32[2,176,352]{2,1,0:T(8,128)S(1)}, f32[2,176,352]{2,1,0:T(8,128)S(1)}, u32[]{:S(2)}, u32[]{:S(2)}) %collective-permute-start.12) | collective-permute-done | bytes 495648 | tf_op jit(solution)/shard_map/ppermute | solution.py:12
  258.4 8.6 %collective-permute-start.13 = (f32[2,176,704]{2,1,0:T(8,128)S(1)}, f32[2,176,704]{2,1,0:T(8,128)}, u32[]{:S(2)}, u32[]{:S(2)}) collective-permute-start(f32[2,176,704]{2,1,0:T(8,128)S(1)} %copy.26), channel_id=1, source_target_pairs={{0,64},{8,72},{16,80},{24,88},{32,96},{40,104},{48,112},{56,120},{... | collective-permute-start | bytes 2973704 | tf_op jit(solution)/shard_map/ppermute | solution.py:12
  267.0 44.9 %collective-permute-done.13 = f32[2,176,704]{2,1,0:T(8,128)} collective-permute-done((f32[2,176,704]{2,1,0:T(8,128)S(1)}, f32[2,176,704]{2,1,0:T(8,128)}, u32[]{:S(2)}, u32[]{:S(2)}) %collective-permute-start.13) | collective-permute-done | bytes 991264 | tf_op jit(solution)/shard_map/ppermute | solution.py:12
  315.2 2.2 convolution_subtract_fusion.2
  317.5 47.1 %reduce-scatter.7.cloned.1.call-done = f32[176,88]{1,0:T(8,128)} async-done(((f32[1408,88]{1,0:T(8,128)}), f32[176,88]{1,0:T(8,128)}) %reduce-scatter.7.cloned.1.call-update) | async-done | bytes 61968 | tf_op jit(solution)/shard_map/reduce_scatter | solution.py:47
  364.6 2.4 collective-permute-start.14
  366.9 4.3 collective-permute-done.14
  372.3 4.0 collective-permute-start.15
  376.3 4.9 collective-permute-done.15
  381.4 3.5 collective-permute-start.16
  384.9 6.4 collective-permute-done.16
  391.6 4.4 collective-permute-start.17
  396.0 14.6 %all_gather.10 = f32[1408,176]{1,0:T(8,128)S(1)} all-gather(f32[176,176]{1,0:T(8,128)S(1)} %copy-done.5), channel_id=1, replica_groups=mesh['leaf'=64,'front'=8] {'front'}, dimensions={0}, use_global_device_ids=true | all-gather | bytes 1115136 | tf_op jit(solution)/shard_map/all_gather | solution.py:69
  413.7 3.4 collective-permute-start.18
  417.1 7.4 %collective-permute-done.18 = f32[2,176,176]{2,1,0:T(8,128)S(1)} collective-permute-done((f32[2,176,176]{2,1,0:T(8,128)S(1)}, f32[2,176,176]{2,1,0:T(8,128)S(1)}, u32[]{:S(2)}, u32[]{:S(2)}) %collective-permute-start.18) | collective-permute-done | bytes 247840 | tf_op jit(solution)/shard_map/ppermute | solution.py:12
  424.7 4.1 collective-permute-start.19
  428.8 11.1 %collective-permute-done.19 = f32[2,176,352]{2,1,0:T(8,128)S(1)} collective-permute-done((f32[2,176,352]{2,1,0:T(8,128)S(1)}, f32[2,176,352]{2,1,0:T(8,128)S(1)}, u32[]{:S(2)}, u32[]{:S(2)}) %collective-permute-start.19) | collective-permute-done | bytes 495648 | tf_op jit(solution)/shard_map/ppermute | solution.py:12
  440.4 2.2 collective-permute-start.20
  442.6 22.2 %collective-permute-done.20 = f32[2,176,704]{2,1,0:T(8,128)S(1)} collective-permute-done((f32[2,176,704]{2,1,0:T(8,128)S(1)}, f32[2,176,704]{2,1,0:T(8,128)S(1)}, u32[]{:S(2)}, u32[]{:S(2)}) %collective-permute-start.20) | collective-permute-done | bytes 991264 | tf_op jit(solution)/shard_map/ppermute | solution.py:12
  465.4 2.4 fusion.2
  467.8 3.5 convolution_subtract_fusion.1
  472.0 49.3 %reduce-scatter.9.cloned.1.call-done = f32[176,176]{1,0:T(8,128)} async-done(((f32[1408,176]{1,0:T(8,128)}), f32[176,176]{1,0:T(8,128)}) %reduce-scatter.9.cloned.1.call-update) | async-done | bytes 123920 | tf_op jit(solution)/shard_map/reduce_scatter | solution.py:47
  521.3 2.5 collective-permute-start.21
  523.9 5.1 collective-permute-done.21
  530.1 4.0 collective-permute-start.22
  534.2 5.8 collective-permute-done.22
  540.3 3.7 collective-permute-start.23
  543.9 11.3 %all-gather.2.cloned.1.call-done = f32[1408,352]{1,0:T(8,128)} async-done(((f32[176,352]{1,0:T(8,128)}), f32[1408,352]{1,0:T(8,128)}) %all-gather.2.cloned.1.call-update) | async-done | bytes 1982480 | tf_op jit(solution)/shard_map/all_gather | solution.py:69
  555.3 3.6 convolution_negate_fusion
  559.0 2.7 collective-permute-start.24
  561.7 13.6 %collective-permute-done.24 = f32[2,176,352]{2,1,0:T(8,128)S(1)} collective-permute-done((f32[2,176,352]{2,1,0:T(8,128)S(1)}, f32[2,176,352]{2,1,0:T(8,128)S(1)}, u32[]{:S(2)}, u32[]{:S(2)}) %collective-permute-start.24) | collective-permute-done | bytes 495648 | tf_op jit(solution)/shard_map/ppermute | solution.py:12
  575.8 4.0 collective-permute-start.25
  579.9 24.6 %collective-permute-done.25 = f32[2,176,704]{2,1,0:T(8,128)S(1)} collective-permute-done((f32[2,176,704]{2,1,0:T(8,128)S(1)}, f32[2,176,704]{2,1,0:T(8,128)S(1)}, u32[]{:S(2)}, u32[]{:S(2)}) %collective-permute-start.25) | collective-permute-done | bytes 991264 | tf_op jit(solution)/shard_map/ppermute | solution.py:12
  605.1 2.6 fusion.1
  607.7 4.0 convolution_subtract_fusion
  614.0 39.5 %reduce-scatter.11.cloned.1.call-done = f32[176,352]{1,0:T(8,128)} async-done(((f32[1408,352]{1,0:T(8,128)}), f32[176,352]{1,0:T(8,128)}) %reduce-scatter.11.cloned.1.call-update) | async-done | bytes 247824 | tf_op jit(solution)/shard_map/reduce_scatter | solution.py:47
  (68 shorter events, 21.4 us)
Async XLA Ops:
  7.2 91.7 %copy-start.9 = (f32[176,44]{0,1:T(8,128)S(1)}, f32[176,44]{0,1:T(8,128)}, u32[]{:S(2)}) copy-start(f32[176,44]{0,1:T(8,128)} %param.7) | copy-start | bytes 92932
  7.2 135.6 %reduce-scatter.13.cloned.1.call-start = ((), (), s32[]{:S(2)}) async-start(), calls=%async_computation.8 | async-start | bytes 811008 | tf_op jit(solution)/shard_map/reduce_scatter | solution.py:47
  8.1 10.2 %collective-permute-start = (f32[176,44]{1,0:T(8,128)S(1)}, f32[176,44]{1,0:T(8,128)S(1)}, u32[]{:S(2)}, u32[]{:S(2)}) collective-permute-start(f32[176,44]{1,0:T(8,128)S(1)} %copy.16), channel_id=1, source_target_pairs={{0,8},{8,0},{16,24},{24,16},{32,40},{40,32},{48,56},{56,48},{64,72... | collective-permute-start | bytes 92936 | tf_op jit(solution)/shard_map/ppermute | solution.py:12
  18.5 7.9 %collective-permute-start.1 = (f32[176,88]{1,0:T(8,128)S(1)}, f32[176,88]{1,0:T(8,128)S(1)}, u32[]{:S(2)}, u32[]{:S(2)}) collective-permute-start(f32[176,88]{1,0:T(8,128)S(1)} %maximum_select_fusion.28), channel_id=1, source_target_pairs={{0,16},{8,24},{16,0},{24,8},{32,48},{40,56},{48,32},{56,40},{64,80... | collective-permute-start | bytes 185864 | tf_op jit(solution)/shard_map/ppermute | solution.py:12
  26.6 8.6 %collective-permute-start.2 = (f32[176,176]{1,0:T(8,128)S(1)}, f32[176,176]{1,0:T(8,128)S(1)}, u32[]{:S(2)}, u32[]{:S(2)}) collective-permute-start(f32[176,176]{1,0:T(8,128)S(1)} %maximum_select_fusion.25), channel_id=1, source_target_pairs={{0,32},{8,40},{16,48},{24,56},{32,0},{40,8},{48,16},{56,24},{64,96... | collective-permute-start | bytes 371720 | tf_op jit(solution)/shard_map/ppermute | solution.py:12
  35.4 11.1 %collective-permute-start.3 = (f32[176,352]{1,0:T(8,128)S(1)}, f32[176,352]{1,0:T(8,128)S(1)}, u32[]{:S(2)}, u32[]{:S(2)}) collective-permute-start(f32[176,352]{1,0:T(8,128)S(1)} %maximum_select_fusion.21), channel_id=1, source_target_pairs={{0,64},{8,72},{16,80},{24,88},{32,96},{40,104},{48,112},{56,120},{... | collective-permute-start | bytes 743432 | tf_op jit(solution)/shard_map/ppermute | solution.py:12
  46.8 52.1 %collective-permute-start.4 = (f32[176,704]{1,0:T(8,128)S(1)}, f32[176,704]{1,0:T(8,128)S(1)}, u32[]{:S(2)}, u32[]{:S(2)}) collective-permute-start(f32[176,704]{1,0:T(8,128)S(1)} %maximum_select_fusion.15), channel_id=1, source_target_pairs={{0,128},{8,136},{16,144},{24,152},{32,160},{40,168},{48,176},{56,1... | collective-permute-start | bytes 1486856 | tf_op jit(solution)/shard_map/ppermute | solution.py:12
  102.4 99.8 %copy-start.7 = (f32[176,88]{1,0:T(8,128)S(1)}, f32[176,88]{1,0:T(8,128)}, u32[]{:S(2)}) copy-start(f32[176,88]{1,0:T(8,128)} %param.11) | copy-start | bytes 185860
  102.5 99.9 %copy-start.6 = (f32[176,88]{1,0:T(8,128)S(1)}, f32[176,88]{1,0:T(8,128)}, u32[]{:S(2)}) copy-start(f32[176,88]{1,0:T(8,128)} %param.8) | copy-start | bytes 185860
  102.5 262.1 %reduce-scatter.7.cloned.1.call-start = ((), (), s32[]{:S(2)}) async-start(), calls=%async_computation.4 | async-start | bytes 811008 | tf_op jit(solution)/shard_map/reduce_scatter | solution.py:47
  142.7 6.6 %collective-permute-start.5 = (f32[176,44]{1,0:T(8,128)}, f32[176,44]{1,0:T(8,128)S(1)}, u32[]{:S(2)}, u32[]{:S(2)}) collective-permute-start(f32[176,44]{1,0:T(8,128)} %reduce-scatter.13.cloned.1.call-done), channel_id=1, source_target_pairs={{0,8},{8,0},{16,24},{24,16},{32,40},{40,32},{48,56},{56,48},{64,72... | collective-permute-start | bytes 92936 | tf_op jit(solution)/shard_map/ppermute | solution.py:12
  150.5 7.9 %collective-permute-start.6 = (f32[176,88]{1,0:T(8,128)S(1)}, f32[176,88]{1,0:T(8,128)S(1)}, u32[]{:S(2)}, u32[]{:S(2)}) collective-permute-start(f32[176,88]{1,0:T(8,128)S(1)} %maximum_select_fusion.29), channel_id=1, source_target_pairs={{0,16},{8,24},{16,0},{24,8},{32,48},{40,56},{48,32},{56,40},{64,80... | collective-permute-start | bytes 185864 | tf_op jit(solution)/shard_map/ppermute | solution.py:12
  158.6 9.0 %collective-permute-start.7 = (f32[176,176]{1,0:T(8,128)S(1)}, f32[176,176]{1,0:T(8,128)S(1)}, u32[]{:S(2)}, u32[]{:S(2)}) collective-permute-start(f32[176,176]{1,0:T(8,128)S(1)} %maximum_select_fusion.26), channel_id=1, source_target_pairs={{0,32},{8,40},{16,48},{24,56},{32,0},{40,8},{48,16},{56,24},{64,96... | collective-permute-start | bytes 371720 | tf_op jit(solution)/shard_map/ppermute | solution.py:12
  167.7 12.1 %collective-permute-start.8 = (f32[176,352]{1,0:T(8,128)S(1)}, f32[176,352]{1,0:T(8,128)S(1)}, u32[]{:S(2)}, u32[]{:S(2)}) collective-permute-start(f32[176,352]{1,0:T(8,128)S(1)} %maximum_select_fusion.22), channel_id=1, source_target_pairs={{0,64},{8,72},{16,80},{24,88},{32,96},{40,104},{48,112},{56,120},{... | collective-permute-start | bytes 743432 | tf_op jit(solution)/shard_map/ppermute | solution.py:12
  180.0 45.9 %collective-permute-start.9 = (f32[176,704]{1,0:T(8,128)S(1)}, f32[176,704]{1,0:T(8,128)S(1)}, u32[]{:S(2)}, u32[]{:S(2)}) collective-permute-start(f32[176,704]{1,0:T(8,128)S(1)} %maximum_select_fusion.16), channel_id=1, source_target_pairs={{0,128},{8,136},{16,144},{24,152},{32,160},{40,168},{48,176},{56,1... | collective-permute-start | bytes 1486856 | tf_op jit(solution)/shard_map/ppermute | solution.py:12
  227.7 7.4 %collective-permute-start.10 = (f32[2,176,88]{1,2,0:T(8,128)S(1)}, f32[2,176,88]{1,2,0:T(8,128)S(1)}, u32[]{:S(2)}, u32[]{:S(2)}) collective-permute-start(f32[2,176,88]{1,2,0:T(8,128)S(1)} %pad_maximum_fusion.2), channel_id=1, source_target_pairs={{0,8},{8,0},{16,24},{24,16},{32,40},{40,32},{48,56},{56,48},{64,72... | collective-permute-start | bytes 371720 | tf_op jit(solution)/shard_map/ppermute | solution.py:12
  235.1 10.8 %collective-permute-start.11 = (f32[2,176,176]{1,2,0:T(8,128)S(1)}, f32[2,176,176]{1,2,0:T(8,128)S(1)}, u32[]{:S(2)}, u32[]{:S(2)}) collective-permute-start(f32[2,176,176]{1,2,0:T(8,128)S(1)} %maximum_select_fusion.20), channel_id=1, source_target_pairs={{0,16},{8,24},{16,0},{24,8},{32,48},{40,56},{48,32},{56,40},{64,80... | collective-permute-start | bytes 743432 | tf_op jit(solution)/shard_map/ppermute | solution.py:12
  246.3 11.3 %collective-permute-start.12 = (f32[2,176,352]{2,1,0:T(8,128)S(1)}, f32[2,176,352]{2,1,0:T(8,128)S(1)}, u32[]{:S(2)}, u32[]{:S(2)}) collective-permute-start(f32[2,176,352]{2,1,0:T(8,128)S(1)} %copy.23), channel_id=1, source_target_pairs={{0,32},{8,40},{16,48},{24,56},{32,0},{40,8},{48,16},{56,24},{64,96... | collective-permute-start | bytes 1486856 | tf_op jit(solution)/shard_map/ppermute | solution.py:12
  258.4 53.5 %collective-permute-start.13 = (f32[2,176,704]{2,1,0:T(8,128)S(1)}, f32[2,176,704]{2,1,0:T(8,128)}, u32[]{:S(2)}, u32[]{:S(2)}) collective-permute-start(f32[2,176,704]{2,1,0:T(8,128)S(1)} %copy.26), channel_id=1, source_target_pairs={{0,64},{8,72},{16,80},{24,88},{32,96},{40,104},{48,112},{56,120},{... | collective-permute-start | bytes 2973704 | tf_op jit(solution)/shard_map/ppermute | solution.py:12
  317.4 78.6 %copy-start.5 = (f32[176,176]{1,0:T(8,128)S(1)}, f32[176,176]{1,0:T(8,128)}, u32[]{:S(2)}) copy-start(f32[176,176]{1,0:T(8,128)} %param.9) | copy-start | bytes 371716
  317.4 203.9 %reduce-scatter.9.cloned.1.call-start = ((), (), s32[]{:S(2)}) async-start(), calls=%async_computation.5 | async-start | bytes 1622016 | tf_op jit(solution)/shard_map/reduce_scatter | solution.py:47
  364.6 6.6 %collective-permute-start.14 = (f32[176,88]{1,0:T(8,128)}, f32[176,88]{1,0:T(8,128)S(1)}, u32[]{:S(2)}, u32[]{:S(2)}) collective-permute-start(f32[176,88]{1,0:T(8,128)} %reduce-scatter.7.cloned.1.call-done), channel_id=1, source_target_pairs={{0,8},{8,0},{16,24},{24,16},{32,40},{40,32},{48,56},{56,48},{64,72... | collective-permute-start | bytes 185864 | tf_op jit(solution)/shard_map/ppermute | solution.py:12
  372.3 8.9 %collective-permute-start.15 = (f32[176,176]{1,0:T(8,128)S(1)}, f32[176,176]{1,0:T(8,128)S(1)}, u32[]{:S(2)}, u32[]{:S(2)}) collective-permute-start(f32[176,176]{1,0:T(8,128)S(1)} %maximum_select_fusion.27), channel_id=1, source_target_pairs={{0,16},{8,24},{16,0},{24,8},{32,48},{40,56},{48,32},{56,40},{64,80... | collective-permute-start | bytes 371720 | tf_op jit(solution)/shard_map/ppermute | solution.py:12
  381.4 9.9 %collective-permute-start.16 = (f32[176,352]{1,0:T(8,128)S(1)}, f32[176,352]{1,0:T(8,128)S(1)}, u32[]{:S(2)}, u32[]{:S(2)}) collective-permute-start(f32[176,352]{1,0:T(8,128)S(1)} %maximum_select_fusion.23), channel_id=1, source_target_pairs={{0,32},{8,40},{16,48},{24,56},{32,0},{40,8},{48,16},{56,24},{64,96... | collective-permute-start | bytes 743432 | tf_op jit(solution)/shard_map/ppermute | solution.py:12
  391.6 20.8 %collective-permute-start.17 = (f32[176,704]{1,0:T(8,128)S(1)}, f32[176,704]{1,0:T(8,128)S(1)}, u32[]{:S(2)}, u32[]{:S(2)}) collective-permute-start(f32[176,704]{1,0:T(8,128)S(1)} %maximum_select_fusion.17), channel_id=1, source_target_pairs={{0,64},{8,72},{16,80},{24,88},{32,96},{40,104},{48,112},{56,120},{... | collective-permute-start | bytes 1486856 | tf_op jit(solution)/shard_map/ppermute | solution.py:12
  410.6 3.1 copy-start.2
  413.7 26.7 %copy-start.3 = (f32[176,176]{1,0:T(8,128)}, f32[176,176]{1,0:T(8,128)S(1)}, u32[]{:S(2)}) copy-start(f32[176,176]{1,0:T(8,128)S(1)} %convolution_negate_fusion.1) | copy-start | bytes 371716
  413.7 10.8 %collective-permute-start.18 = (f32[2,176,176]{2,1,0:T(8,128)S(1)}, f32[2,176,176]{2,1,0:T(8,128)S(1)}, u32[]{:S(2)}, u32[]{:S(2)}) collective-permute-start(f32[2,176,176]{2,1,0:T(8,128)S(1)} %pad_maximum_fusion.1), channel_id=1, source_target_pairs={{0,8},{8,0},{16,24},{24,16},{32,40},{40,32},{48,56},{56,48},{64,72... | collective-permute-start | bytes 743432 | tf_op jit(solution)/shard_map/ppermute | solution.py:12
  424.7 15.2 %collective-permute-start.19 = (f32[2,176,352]{2,1,0:T(8,128)S(1)}, f32[2,176,352]{2,1,0:T(8,128)S(1)}, u32[]{:S(2)}, u32[]{:S(2)}) collective-permute-start(f32[2,176,352]{2,1,0:T(8,128)S(1)} %maximum_select_fusion.18), channel_id=1, source_target_pairs={{0,16},{8,24},{16,0},{24,8},{32,48},{40,56},{48,32},{56,40},{64,80... | collective-permute-start | bytes 1486856 | tf_op jit(solution)/shard_map/ppermute | solution.py:12
  440.4 24.4 %collective-permute-start.20 = (f32[2,176,704]{2,1,0:T(8,128)S(1)}, f32[2,176,704]{2,1,0:T(8,128)S(1)}, u32[]{:S(2)}, u32[]{:S(2)}) collective-permute-start(f32[2,176,704]{2,1,0:T(8,128)S(1)} %maximum_select_fusion.4), channel_id=1, source_target_pairs={{0,32},{8,40},{16,48},{24,56},{32,0},{40,8},{48,16},{56,24},{64,96... | collective-permute-start | bytes 2973704 | tf_op jit(solution)/shard_map/ppermute | solution.py:12
  471.4 83.8 %all-gather.2.cloned.1.call-start = ((), (), s32[]{:S(2)}) async-start(), calls=%async_computation.6 | async-start | bytes 2433024 | tf_op jit(solution)/shard_map/all_gather | solution.py:69
  472.0 181.5 %reduce-scatter.11.cloned.1.call-start = ((), (), s32[]{:S(2)}) async-start(), calls=%async_computation.7 | async-start | bytes 2433024 | tf_op jit(solution)/shard_map/reduce_scatter | solution.py:47
  521.3 7.6 %collective-permute-start.21 = (f32[176,176]{1,0:T(8,128)}, f32[176,176]{1,0:T(8,128)S(1)}, u32[]{:S(2)}, u32[]{:S(2)}) collective-permute-start(f32[176,176]{1,0:T(8,128)} %reduce-scatter.9.cloned.1.call-done), channel_id=1, source_target_pairs={{0,8},{8,0},{16,24},{24,16},{32,40},{40,32},{48,56},{56,48},{64,72... | collective-permute-start | bytes 371720 | tf_op jit(solution)/shard_map/ppermute | solution.py:12
  530.1 9.9 %collective-permute-start.22 = (f32[176,352]{1,0:T(8,128)S(1)}, f32[176,352]{1,0:T(8,128)S(1)}, u32[]{:S(2)}, u32[]{:S(2)}) collective-permute-start(f32[176,352]{1,0:T(8,128)S(1)} %maximum_select_fusion.24), channel_id=1, source_target_pairs={{0,16},{8,24},{16,0},{24,8},{32,48},{40,56},{48,32},{56,40},{64,80... | collective-permute-start | bytes 743432 | tf_op jit(solution)/shard_map/ppermute | solution.py:12
  540.3 18.7 %copy-start.1 = (f32[176,352]{1,0:T(8,128)S(1)}, f32[176,352]{1,0:T(8,128)}, u32[]{:S(2)}) copy-start(f32[176,352]{1,0:T(8,128)} %param.13) | copy-start | bytes 743428
  540.3 15.0 %collective-permute-start.23 = (f32[176,704]{1,0:T(8,128)S(1)}, f32[176,704]{1,0:T(8,128)S(1)}, u32[]{:S(2)}, u32[]{:S(2)}) collective-permute-start(f32[176,704]{1,0:T(8,128)S(1)} %maximum_select_fusion.19), channel_id=1, source_target_pairs={{0,32},{8,40},{16,48},{24,56},{32,0},{40,8},{48,16},{56,24},{64,96... | collective-permute-start | bytes 1486856 | tf_op jit(solution)/shard_map/ppermute | solution.py:12
  558.9 16.9 %copy-start = (f32[176,352]{1,0:T(8,128)}, f32[176,352]{1,0:T(8,128)S(1)}, u32[]{:S(2)}) copy-start(f32[176,352]{1,0:T(8,128)S(1)} %convolution_negate_fusion) | copy-start | bytes 743428
  559.0 16.3 %collective-permute-start.24 = (f32[2,176,352]{2,1,0:T(8,128)S(1)}, f32[2,176,352]{2,1,0:T(8,128)S(1)}, u32[]{:S(2)}, u32[]{:S(2)}) collective-permute-start(f32[2,176,352]{2,1,0:T(8,128)S(1)} %pad_maximum_fusion), channel_id=1, source_target_pairs={{0,8},{8,0},{16,24},{24,16},{32,40},{40,32},{48,56},{56,48},{64,72... | collective-permute-start | bytes 1486856 | tf_op jit(solution)/shard_map/ppermute | solution.py:12
  575.8 28.6 %collective-permute-start.25 = (f32[2,176,704]{2,1,0:T(8,128)S(1)}, f32[2,176,704]{2,1,0:T(8,128)S(1)}, u32[]{:S(2)}, u32[]{:S(2)}) collective-permute-start(f32[2,176,704]{2,1,0:T(8,128)S(1)} %maximum_select_fusion.5), channel_id=1, source_target_pairs={{0,16},{8,24},{16,0},{24,8},{32,48},{40,56},{48,32},{56,40},{64,80... | collective-permute-start | bytes 2973704 | tf_op jit(solution)/shard_map/ppermute | solution.py:12
  605.1 2.6 copy-start.4
  611.6 0.9 copy-start.8
Sparse Core Ops, SparseCore 0:
  102.6 40.1 reduce-scatter.12
  317.6 46.9 reduce-scatter.6
  471.5 49.7 reduce-scatter.8
  523.3 31.8 all-gather.1
  611.8 41.6 reduce-scatter.10
where the time goes:
time: 661 us; the launch traced here: 660 us
  waiting for transfers between devices  461 us (70%)
  starting transfers between devices  115 us (17%)
  blocking collectives  27.9 us (4%)
  matrix products  26.2 us (4%)
  between operations  14.4 us (2%)
  other arithmetic  8.58 us (1%)
    ppermute x26, waiting for transfers between devices, from_partner(): return lax.ppermute(value, axis, pairs)  274 us
    reduce_scatter x4, waiting for transfers between devices, front_sum(): lax.psum_scatter(term_fn(jnp.int32(0), share_rows * lax.axis_size('front'...  176 us
    ppermute x26, starting transfers between devices, from_partner(): return lax.ppermute(value, axis, pairs)  115 us
    all_gather x2, blocking collectives, local(): lax.all_gather(panel_tile, 'front', axis=0, tiled=True)  27.9 us
    dot_general x6, matrix products, inner_product(): lax.dot_general(first, second, (((0,), (0,)), ((), ())), precision=lax.Pr...  15.9 us
  transfers between devices with their start and end apart: 31, of which 30 were waited for; matrix products, arithmetic and copies ran while one was open for 0% of the time, Pallas kernels for 0%

commit v1 on v0

--- a/solution.py
+++ b/solution.py
@@ -4,6 +4,25 @@
 from jax.sharding import PartitionSpec as P
 
 S = 1408
+
+
+def try_all_terms(field_in, peer_axis, d_out):
+    full_n = lax.psum(1, peer_axis)
+    entries = [(k0, (k0 + 1) % full_n) for k0 in range(full_n)]
+    mixed_arr, arr_out = ([field_in], [field_in])
+    by_rank = [(k0, (k0 - 1) % full_n) for k0 in range(full_n)]
+    for _ in range(full_n // 2):
+        seen_now = lax.ppermute(mixed_arr[-1], peer_axis, entries)
+        mixed_arr.append(seen_now)
+    for _ in [*range((full_n - 1) // 2)]:
+        piece_now = lax.ppermute(arr_out[-1], peer_axis, by_rank)
+        arr_out.append(piece_now)
+    block_out = jnp.concatenate([*mixed_arr[::-1], *arr_out[1:]], axis=d_out)
+    return jnp.roll(
+        block_out,
+        shift=(lax.axis_index(peer_axis) - full_n // 2) * field_in.shape[d_out],
+        axis=d_out,
+    )
 
 
 def from_partner(value, axis, distance):
@@ -66,7 +85,7 @@
         tile_width = panel_tile.shape[1]
         cube_size = S // tile_width
         parent_rows = cube_rows(parent, S // parent.shape[1])
-        cross_block = -product(parent_rows, lax.all_gather(panel_tile, "front", axis=0, tiled=True))
+        cross_block = -product(parent_rows, try_all_terms(panel_tile, "front", 0))
         stacked = cube_rows(jnp.stack([cross_block, factor_tile]), cube_size)
 
         def level_term(offset, amount):

time: 661 us -> 661 us (level)
  starting transfers between devices: 115 us -> 150 us
  blocking collectives: 27.9 us -> 0 us
  waiting for transfers between devices: 461 us -> 437 us
  local copies, waits for them, and re-layouts: 5.99 us -> 23.2 us
    reduce_scatter x4, waiting for transfers between devices: 176 us -> 119 us  [front_sum(): lax.psum_scatter(term_fn(jnp.int32(0), share_rows * lax.axis_size('front'...]
    ppermute x0 -> x21, waiting for transfers between devices: none -> 45.7 us  [the longest x12 45.7 us: try_all_terms(): seen_now = lax.ppermute(mixed_arr[-1], peer_axis, entries)]
    ppermute x0 -> x21, starting transfers between devices: none -> 35.7 us  [the longest x9 35.6 us: try_all_terms(): piece_now = lax.ppermute(arr_out[-1], peer_axis, by_rank)]
    all_gather x2 -> x0, blocking collectives: 27.9 us -> none  [local(): lax.all_gather(panel_tile, 'front', axis=0, tiled=True)]
    unnamed x24 -> x85, local copies, waits for them, and re-layouts: 3.36 us -> 18.9 us
    all_gather x1 -> x0, waiting for transfers between devices: 11.3 us -> none  [local(): lax.all_gather(panel_tile, 'front', axis=0, tiled=True)]
  transfers between devices with their start and end apart: 31 -> 51, of which waited for: 30 -> 40; matrix products, arithmetic and copies ran while one was open for 0% -> 5% of each run, Pallas kernels for 0% -> 0%
where the time goes in v1:
time: 661 us; the launch traced here: 660 us
  waiting for transfers between devices  437 us (66%)
  starting transfers between devices  150 us (23%)
  matrix products  26.7 us (4%)
  local copies, waits for them, and re-layouts  23.2 us (4%)
  between operations  14.8 us (2%)
  other arithmetic  8.54 us (1%)
    ppermute x26, waiting for transfers between devices, from_partner(): return lax.ppermute(value, axis, pairs)  272 us
    reduce_scatter x4, waiting for transfers between devices, front_sum(): lax.psum_scatter(term_fn(jnp.int32(0), share_rows * lax.axis_size('front'...  119 us
    ppermute x26, starting transfers between devices, from_partner(): return lax.ppermute(value, axis, pairs)  114 us
    ppermute x12, waiting for transfers between devices, try_all_terms(): seen_now = lax.ppermute(mixed_arr[-1], peer_axis, entries)  45.7 us
    ppermute x9, starting transfers between devices, try_all_terms(): piece_now = lax.ppermute(arr_out[-1], peer_axis, by_rank)  35.6 us
    unnamed x85, local copies, waits for them, and re-layouts  18.9 us
    dot_general x6, matrix products, inner_product(): lax.dot_general(first, second, (((0,), (0,)), ((), ())), precision=lax.Pr...  16.2 us
  transfers between devices with their start and end apart: 51, of which 40 were waited for; matrix products, arithmetic and copies ran while one was open for 5% of the time, Pallas kernels for 0%

profile of v1, /device:TPU:8, one launch (start us, length us, event | category | flops | bytes accessed | tf_op | source)
XLA Modules:
  0.0 660.1 jit_solution(686576142577961919)
XLA Ops:
  8.1 7.7 %collective-permute-start = (f32[176,44]{1,0:T(8,128)S(1)}, f32[176,44]{1,0:T(8,128)S(1)}, u32[]{:S(2)}, u32[]{:S(2)}) collective-permute-start(f32[176,44]{1,0:T(8,128)S(1)} %copy.16), channel_id=1, source_target_pairs={{0,8},{8,0},{16,24},{24,16},{32,40},{40,32},{48,56},{56,48},{64,72... | collective-permute-start | bytes 92936 | tf_op jit(solution)/shard_map/ppermute | solution.py:31
  20.4 6.0 collective-permute-done.1
  28.5 6.7 %collective-permute-done.2 = f32[176,176]{1,0:T(8,128)S(1)} collective-permute-done((f32[176,176]{1,0:T(8,128)S(1)}, f32[176,176]{1,0:T(8,128)S(1)}, u32[]{:S(2)}, u32[]{:S(2)}) %collective-permute-start.2) | collective-permute-done | bytes 123936 | tf_op jit(solution)/shard_map/ppermute | solution.py:31
  37.5 9.2 %collective-permute-done.3 = f32[176,352]{1,0:T(8,128)S(1)} collective-permute-done((f32[176,352]{1,0:T(8,128)S(1)}, f32[176,352]{1,0:T(8,128)S(1)}, u32[]{:S(2)}, u32[]{:S(2)}) %collective-permute-start.3) | collective-permute-done | bytes 247840 | tf_op jit(solution)/shard_map/ppermute | solution.py:31
  46.9 7.1 %collective-permute-start.4 = (f32[176,704]{1,0:T(8,128)S(1)}, f32[176,704]{1,0:T(8,128)S(1)}, u32[]{:S(2)}, u32[]{:S(2)}) collective-permute-start(f32[176,704]{1,0:T(8,128)S(1)} %maximum_select_fusion.15), channel_id=1, source_target_pairs={{0,128},{8,136},{16,144},{24,152},{32,160},{40,168},{48,176},{56,1... | collective-permute-start | bytes 1486856 | tf_op jit(solution)/shard_map/ppermute | solution.py:31
  54.1 5.2 collective-permute-done.10
  59.2 3.0 collective-permute-start.14
  64.4 3.0 collective-permute-start.15
  69.6 29.4 %collective-permute-done.4 = f32[176,704]{1,0:T(8,128)S(1)} collective-permute-done((f32[176,704]{1,0:T(8,128)S(1)}, f32[176,704]{1,0:T(8,128)S(1)}, u32[]{:S(2)}, u32[]{:S(2)}) %collective-permute-start.4) | collective-permute-done | bytes 495648 | tf_op jit(solution)/shard_map/ppermute | solution.py:31
  99.0 3.6 fusion.13
  105.3 37.6 %reduce-scatter.13.cloned.1.call-done = f32[176,44]{1,0:T(8,128)} async-done(((f32[1408,44]{1,0:T(8,128)}), f32[176,44]{1,0:T(8,128)}) %reduce-scatter.13.cloned.1.call-update) | async-done | bytes 30992 | tf_op jit(solution)/shard_map/reduce_scatter | solution.py:66
  145.4 4.2 collective-permute-done.5
  150.7 4.0 collective-permute-start.6
  154.7 3.9 collective-permute-done.6
  158.7 3.4 collective-permute-start.7
  162.2 5.5 collective-permute-done.7
  167.9 4.4 collective-permute-start.8
  172.4 7.6 %collective-permute-done.8 = f32[176,352]{1,0:T(8,128)S(1)} collective-permute-done((f32[176,352]{1,0:T(8,128)S(1)}, f32[176,352]{1,0:T(8,128)S(1)}, u32[]{:S(2)}, u32[]{:S(2)}) %collective-permute-start.8) | collective-permute-done | bytes 247840 | tf_op jit(solution)/shard_map/ppermute | solution.py:31
  180.2 22.2 %collective-permute-start.9 = (f32[176,704]{1,0:T(8,128)S(1)}, f32[176,704]{1,0:T(8,128)S(1)}, u32[]{:S(2)}, u32[]{:S(2)}) collective-permute-start(f32[176,704]{1,0:T(8,128)S(1)} %maximum_select_fusion.16), channel_id=1, source_target_pairs={{0,128},{8,136},{16,144},{24,152},{32,160},{40,168},{48,176},{56,1... | collective-permute-start | bytes 1486856 | tf_op jit(solution)/shard_map/ppermute | solution.py:31
  202.6 23.6 %collective-permute-done.9 = f32[176,704]{1,0:T(8,128)S(1)} collective-permute-done((f32[176,704]{1,0:T(8,128)S(1)}, f32[176,704]{1,0:T(8,128)S(1)}, u32[]{:S(2)}, u32[]{:S(2)}) %collective-permute-start.9) | collective-permute-done | bytes 495648 | tf_op jit(solution)/shard_map/ppermute | solution.py:31
  230.8 4.5 collective-permute-done.17
  235.4 4.0 collective-permute-start.18
  239.4 6.8 %collective-permute-done.18 = f32[2,176,176]{1,2,0:T(8,128)S(1)} collective-permute-done((f32[2,176,176]{1,2,0:T(8,128)S(1)}, f32[2,176,176]{1,2,0:T(8,128)S(1)}, u32[]{:S(2)}, u32[]{:S(2)}) %collective-permute-start.18) | collective-permute-done | bytes 247840 | tf_op jit(solution)/shard_map/ppermute | solution.py:31
  248.4 9.3 %collective-permute-done.19 = f32[2,176,352]{2,1,0:T(8,128)S(1)} collective-permute-done((f32[2,176,352]{2,1,0:T(8,128)S(1)}, f32[2,176,352]{2,1,0:T(8,128)S(1)}, u32[]{:S(2)}, u32[]{:S(2)}) %collective-permute-start.19) | collective-permute-done | bytes 495648 | tf_op jit(solution)/shard_map/ppermute | solution.py:31
  258.7 8.6 %collective-permute-start.20 = (f32[2,176,704]{2,1,0:T(8,128)S(1)}, f32[2,176,704]{2,1,0:T(8,128)}, u32[]{:S(2)}, u32[]{:S(2)}) collective-permute-start(f32[2,176,704]{2,1,0:T(8,128)S(1)} %copy.26), channel_id=1, source_target_pairs={{0,64},{8,72},{16,80},{24,88},{32,96},{40,104},{48,112},{56,120},{... | collective-permute-start | bytes 2973704 | tf_op jit(solution)/shard_map/ppermute | solution.py:31
  267.2 44.9 %collective-permute-done.20 = f32[2,176,704]{2,1,0:T(8,128)} collective-permute-done((f32[2,176,704]{2,1,0:T(8,128)S(1)}, f32[2,176,704]{2,1,0:T(8,128)}, u32[]{:S(2)}, u32[]{:S(2)}) %collective-permute-start.20) | collective-permute-done | bytes 991264 | tf_op jit(solution)/shard_map/ppermute | solution.py:31
  318.0 12.4 %collective-permute-start.29 = (f32[176,176]{1,0:T(8,128)S(1)}, f32[176,176]{1,0:T(8,128)S(1)}, u32[]{:S(2)}, u32[]{:S(2)}) collective-permute-start(f32[176,176]{1,0:T(8,128)S(1)} %copy-done.3), channel_id=1, source_target_pairs={{0,7},{1,0},{2,1},{3,2},{4,3},{5,4},{6,5},{7,6},{8,15},{9,8},{10,9... | collective-permute-start | bytes 371720 | tf_op jit(solution)/shard_map/ppermute | solution.py:18
  330.4 3.2 collective-permute-done.26
  333.6 3.0 collective-permute-start.30
  336.5 3.2 collective-permute-done.27
  339.7 3.1 collective-permute-start.31
  342.8 3.5 collective-permute-done.28
  347.0 17.9 %reduce-scatter.7.cloned.1.call-done = f32[176,88]{1,0:T(8,128)} async-done(((f32[1408,88]{1,0:T(8,128)}), f32[176,88]{1,0:T(8,128)}) %reduce-scatter.7.cloned.1.call-update) | async-done | bytes 61968 | tf_op jit(solution)/shard_map/reduce_scatter | solution.py:66
  368.5 3.2 collective-permute-done.21
  372.8 3.8 collective-permute-start.22
  378.6 3.1 collective-permute-done.22
  381.9 3.3 collective-permute-start.23
  385.3 6.5 collective-permute-done.23
  392.1 4.3 collective-permute-start.24
  398.3 14.5 %collective-permute-done.24 = f32[176,704]{1,0:T(8,128)S(1)} collective-permute-done((f32[176,704]{1,0:T(8,128)S(1)}, f32[176,704]{1,0:T(8,128)S(1)}, u32[]{:S(2)}, u32[]{:S(2)}) %collective-permute-start.24) | collective-permute-done | bytes 495648 | tf_op jit(solution)/shard_map/ppermute | solution.py:31
  414.2 3.3 collective-permute-start.32
  417.6 7.0 %collective-permute-done.32 = f32[2,176,176]{2,1,0:T(8,128)S(1)} collective-permute-done((f32[2,176,176]{2,1,0:T(8,128)S(1)}, f32[2,176,176]{2,1,0:T(8,128)S(1)}, u32[]{:S(2)}, u32[]{:S(2)}) %collective-permute-start.32) | collective-permute-done | bytes 247840 | tf_op jit(solution)/shard_map/ppermute | solution.py:31
  424.8 3.4 collective-permute-start.33
  428.3 11.3 %collective-permute-done.33 = f32[2,176,352]{2,1,0:T(8,128)S(1)} collective-permute-done((f32[2,176,352]{2,1,0:T(8,128)S(1)}, f32[2,176,352]{2,1,0:T(8,128)S(1)}, u32[]{:S(2)}, u32[]{:S(2)}) %collective-permute-start.33) | collective-permute-done | bytes 495648 | tf_op jit(solution)/shard_map/ppermute | solution.py:31
  442.6 21.4 %collective-permute-done.34 = f32[2,176,704]{2,1,0:T(8,128)S(1)} collective-permute-done((f32[2,176,704]{2,1,0:T(8,128)S(1)}, f32[2,176,704]{2,1,0:T(8,128)S(1)}, u32[]{:S(2)}, u32[]{:S(2)}) %collective-permute-start.34) | collective-permute-done | bytes 991264 | tf_op jit(solution)/shard_map/ppermute | solution.py:31
  467.2 3.7 convolution_subtract_fusion.1
  471.0 12.7 %collective-permute-done.38 = f32[176,352]{1,0:T(8,128)S(1)} collective-permute-done((f32[176,352]{1,0:T(8,128)S(1)}, f32[176,352]{1,0:T(8,128)S(1)}, u32[]{:S(2)}, u32[]{:S(2)}) %collective-permute-start.38) | collective-permute-done | bytes 247840 | tf_op jit(solution)/shard_map/ppermute | solution.py:15
  483.7 3.0 collective-permute-start.42
  486.6 4.1 collective-permute-done.39
  490.8 3.0 collective-permute-start.43
  493.7 4.1 collective-permute-done.40
  500.8 5.3 collective-permute-done.41
  510.5 12.3 %reduce-scatter.9.cloned.1.call-done = f32[176,176]{1,0:T(8,128)} async-done(((f32[1408,176]{1,0:T(8,128)}), f32[176,176]{1,0:T(8,128)}) %reduce-scatter.9.cloned.1.call-update) | async-done | bytes 123920 | tf_op jit(solution)/shard_map/reduce_scatter | solution.py:66
  526.6 3.8 collective-permute-done.35
  531.6 4.0 collective-permute-start.36
  537.7 3.7 collective-permute-done.36
  541.7 3.6 collective-permute-start.37
  549.0 4.1 collective-permute-done.37
  553.0 3.8 fusion.5
  556.9 3.6 collective-permute-start.45
  560.6 9.0 %collective-permute-done.45 = f32[2,176,352]{2,1,0:T(8,128)S(1)} collective-permute-done((f32[2,176,352]{2,1,0:T(8,128)S(1)}, f32[2,176,352]{2,1,0:T(8,128)S(1)}, u32[]{:S(2)}, u32[]{:S(2)}) %collective-permute-start.45) | collective-permute-done | bytes 495648 | tf_op jit(solution)/shard_map/ppermute | solution.py:31
  572.5 20.5 %collective-permute-done.46 = f32[2,176,704]{2,1,0:T(8,128)S(1)} collective-permute-done((f32[2,176,704]{2,1,0:T(8,128)S(1)}, f32[2,176,704]{2,1,0:T(8,128)S(1)}, u32[]{:S(2)}, u32[]{:S(2)}) %collective-permute-start.46) | collective-permute-done | bytes 991264 | tf_op jit(solution)/shard_map/ppermute | solution.py:31
  596.3 3.9 convolution_subtract_fusion
  602.6 51.1 %reduce-scatter.11.cloned.1.call-done = f32[176,352]{1,0:T(8,128)} async-done(((f32[1408,352]{1,0:T(8,128)}), f32[176,352]{1,0:T(8,128)}) %reduce-scatter.11.cloned.1.call-update) | async-done | bytes 247824 | tf_op jit(solution)/shard_map/reduce_scatter | solution.py:66
  (169 shorter events, 79.1 us)
Async XLA Ops:
  7.2 91.8 %copy-start.17 = (f32[176,44]{0,1:T(8,128)S(1)}, f32[176,44]{0,1:T(8,128)}, u32[]{:S(2)}) copy-start(f32[176,44]{0,1:T(8,128)} %param.7) | copy-start | bytes 92932
  7.2 46.9 %copy-start.6 = (f32[176,88]{1,0:T(8,128)S(1)}, f32[176,88]{1,0:T(8,128)}, u32[]{:S(2)}) copy-start(f32[176,88]{1,0:T(8,128)} %param.8) | copy-start | bytes 185860
  7.2 135.8 %reduce-scatter.13.cloned.1.call-start = ((), (), s32[]{:S(2)}) async-start(), calls=%async_computation.7 | async-start | bytes 811008 | tf_op jit(solution)/shard_map/reduce_scatter | solution.py:66
  8.1 10.2 %collective-permute-start = (f32[176,44]{1,0:T(8,128)S(1)}, f32[176,44]{1,0:T(8,128)S(1)}, u32[]{:S(2)}, u32[]{:S(2)}) collective-permute-start(f32[176,44]{1,0:T(8,128)S(1)} %copy.16), channel_id=1, source_target_pairs={{0,8},{8,0},{16,24},{24,16},{32,40},{40,32},{48,56},{56,48},{64,72... | collective-permute-start | bytes 92936 | tf_op jit(solution)/shard_map/ppermute | solution.py:31
  18.5 7.9 %collective-permute-start.1 = (f32[176,88]{1,0:T(8,128)S(1)}, f32[176,88]{1,0:T(8,128)S(1)}, u32[]{:S(2)}, u32[]{:S(2)}) collective-permute-start(f32[176,88]{1,0:T(8,128)S(1)} %maximum_select_fusion.28), channel_id=1, source_target_pairs={{0,16},{8,24},{16,0},{24,8},{32,48},{40,56},{48,32},{56,40},{64,80... | collective-permute-start | bytes 185864 | tf_op jit(solution)/shard_map/ppermute | solution.py:31
  26.6 8.6 %collective-permute-start.2 = (f32[176,176]{1,0:T(8,128)S(1)}, f32[176,176]{1,0:T(8,128)S(1)}, u32[]{:S(2)}, u32[]{:S(2)}) collective-permute-start(f32[176,176]{1,0:T(8,128)S(1)} %maximum_select_fusion.25), channel_id=1, source_target_pairs={{0,32},{8,40},{16,48},{24,56},{32,0},{40,8},{48,16},{56,24},{64,96... | collective-permute-start | bytes 371720 | tf_op jit(solution)/shard_map/ppermute | solution.py:31
  35.4 67.4 %copy-start.15 = (f32[176,88]{1,0:T(8,128)S(1)}, f32[176,88]{1,0:T(8,128)}, u32[]{:S(2)}) copy-start(f32[176,88]{1,0:T(8,128)} %param.11) | copy-start | bytes 185860
  35.4 11.3 %collective-permute-start.3 = (f32[176,352]{1,0:T(8,128)S(1)}, f32[176,352]{1,0:T(8,128)S(1)}, u32[]{:S(2)}, u32[]{:S(2)}) collective-permute-start(f32[176,352]{1,0:T(8,128)S(1)} %maximum_select_fusion.21), channel_id=1, source_target_pairs={{0,64},{8,72},{16,80},{24,88},{32,96},{40,104},{48,112},{56,120},{... | collective-permute-start | bytes 743432 | tf_op jit(solution)/shard_map/ppermute | solution.py:31
  46.9 52.1 %collective-permute-start.4 = (f32[176,704]{1,0:T(8,128)S(1)}, f32[176,704]{1,0:T(8,128)S(1)}, u32[]{:S(2)}, u32[]{:S(2)}) collective-permute-start(f32[176,704]{1,0:T(8,128)S(1)} %maximum_select_fusion.15), channel_id=1, source_target_pairs={{0,128},{8,136},{16,144},{24,152},{32,160},{40,168},{48,176},{56,1... | collective-permute-start | bytes 1486856 | tf_op jit(solution)/shard_map/ppermute | solution.py:31
  54.1 5.2 collective-permute-start.10
  59.2 5.2 collective-permute-start.11
  59.2 5.2 collective-permute-start.14
  64.4 5.2 collective-permute-start.12
  64.4 38.4 %collective-permute-start.15 = (f32[176,88]{1,0:T(8,128)S(1)}, f32[176,88]{1,0:T(8,128)S(1)}, u32[]{:S(2)}, u32[]{:S(2)}) collective-permute-start(f32[176,88]{1,0:T(8,128)S(1)} %collective-permute-done.14), channel_id=1, source_target_pairs={{0,7},{1,0},{2,1},{3,2},{4,3},{5,4},{6,5},{7,6},{8,15},{9,8},{10,9... | collective-permute-start | bytes 185864 | tf_op jit(solution)/shard_map/ppermute | solution.py:18
  69.6 35.7 %collective-permute-start.13 = (f32[176,88]{1,0:T(8,128)S(1)}, f32[176,88]{1,0:T(8,128)S(1)}, u32[]{:S(2)}, u32[]{:S(2)}) collective-permute-start(f32[176,88]{1,0:T(8,128)S(1)} %collective-permute-done.12), channel_id=1, source_target_pairs={{0,1},{1,2},{2,3},{3,4},{4,5},{5,6},{6,7},{7,0},{8,9},{9,10},{10,1... | collective-permute-start | bytes 185864 | tf_op jit(solution)/shard_map/ppermute | solution.py:15
  102.7 262.3 %reduce-scatter.7.cloned.1.call-start = ((), (), s32[]{:S(2)}) async-start(), calls=%async_computation.4 | async-start | bytes 811008 | tf_op jit(solution)/shard_map/reduce_scatter | solution.py:66
  102.9 59.4 %collective-permute-start.16 = (f32[176,88]{1,0:T(8,128)S(1)}, f32[176,88]{1,0:T(8,128)S(1)}, u32[]{:S(2)}, u32[]{:S(2)}) collective-permute-start(f32[176,88]{1,0:T(8,128)S(1)} %collective-permute-done.15), channel_id=1, source_target_pairs={{0,7},{1,0},{2,1},{3,2},{4,3},{5,4},{6,5},{7,6},{8,15},{9,8},{10,9... | collective-permute-start | bytes 185864 | tf_op jit(solution)/shard_map/ppermute | solution.py:18
  142.9 6.6 %collective-permute-start.5 = (f32[176,44]{1,0:T(8,128)}, f32[176,44]{1,0:T(8,128)S(1)}, u32[]{:S(2)}, u32[]{:S(2)}) collective-permute-start(f32[176,44]{1,0:T(8,128)} %reduce-scatter.13.cloned.1.call-done), channel_id=1, source_target_pairs={{0,8},{8,0},{16,24},{24,16},{32,40},{40,32},{48,56},{56,48},{64,72... | collective-permute-start | bytes 92936 | tf_op jit(solution)/shard_map/ppermute | solution.py:31
  150.7 7.9 %collective-permute-start.6 = (f32[176,88]{1,0:T(8,128)S(1)}, f32[176,88]{1,0:T(8,128)S(1)}, u32[]{:S(2)}, u32[]{:S(2)}) collective-permute-start(f32[176,88]{1,0:T(8,128)S(1)} %maximum_select_fusion.29), channel_id=1, source_target_pairs={{0,16},{8,24},{16,0},{24,8},{32,48},{40,56},{48,32},{56,40},{64,80... | collective-permute-start | bytes 185864 | tf_op jit(solution)/shard_map/ppermute | solution.py:31
  158.7 9.0 %collective-permute-start.7 = (f32[176,176]{1,0:T(8,128)S(1)}, f32[176,176]{1,0:T(8,128)S(1)}, u32[]{:S(2)}, u32[]{:S(2)}) collective-permute-start(f32[176,176]{1,0:T(8,128)S(1)} %maximum_select_fusion.26), channel_id=1, source_target_pairs={{0,32},{8,40},{16,48},{24,56},{32,0},{40,8},{48,16},{56,24},{64,96... | collective-permute-start | bytes 371720 | tf_op jit(solution)/shard_map/ppermute | solution.py:31
  167.9 12.1 %collective-permute-start.8 = (f32[176,352]{1,0:T(8,128)S(1)}, f32[176,352]{1,0:T(8,128)S(1)}, u32[]{:S(2)}, u32[]{:S(2)}) collective-permute-start(f32[176,352]{1,0:T(8,128)S(1)} %maximum_select_fusion.22), channel_id=1, source_target_pairs={{0,64},{8,72},{16,80},{24,88},{32,96},{40,104},{48,112},{56,120},{... | collective-permute-start | bytes 743432 | tf_op jit(solution)/shard_map/ppermute | solution.py:31
  180.2 46.0 %collective-permute-start.9 = (f32[176,704]{1,0:T(8,128)S(1)}, f32[176,704]{1,0:T(8,128)S(1)}, u32[]{:S(2)}, u32[]{:S(2)}) collective-permute-start(f32[176,704]{1,0:T(8,128)S(1)} %maximum_select_fusion.16), channel_id=1, source_target_pairs={{0,128},{8,136},{16,144},{24,152},{32,160},{40,168},{48,176},{56,1... | collective-permute-start | bytes 1486856 | tf_op jit(solution)/shard_map/ppermute | solution.py:31
  227.9 7.4 %collective-permute-start.17 = (f32[2,176,88]{1,2,0:T(8,128)S(1)}, f32[2,176,88]{1,2,0:T(8,128)S(1)}, u32[]{:S(2)}, u32[]{:S(2)}) collective-permute-start(f32[2,176,88]{1,2,0:T(8,128)S(1)} %pad_maximum_fusion.2), channel_id=1, source_target_pairs={{0,8},{8,0},{16,24},{24,16},{32,40},{40,32},{48,56},{56,48},{64,72... | collective-permute-start | bytes 371720 | tf_op jit(solution)/shard_map/ppermute | solution.py:31
  235.4 10.8 %collective-permute-start.18 = (f32[2,176,176]{1,2,0:T(8,128)S(1)}, f32[2,176,176]{1,2,0:T(8,128)S(1)}, u32[]{:S(2)}, u32[]{:S(2)}) collective-permute-start(f32[2,176,176]{1,2,0:T(8,128)S(1)} %maximum_select_fusion.20), channel_id=1, source_target_pairs={{0,16},{8,24},{16,0},{24,8},{32,48},{40,56},{48,32},{56,40},{64,80... | collective-permute-start | bytes 743432 | tf_op jit(solution)/shard_map/ppermute | solution.py:31
  246.5 11.3 %collective-permute-start.19 = (f32[2,176,352]{2,1,0:T(8,128)S(1)}, f32[2,176,352]{2,1,0:T(8,128)S(1)}, u32[]{:S(2)}, u32[]{:S(2)}) collective-permute-start(f32[2,176,352]{2,1,0:T(8,128)S(1)} %copy.23), channel_id=1, source_target_pairs={{0,32},{8,40},{16,48},{24,56},{32,0},{40,8},{48,16},{56,24},{64,96... | collective-permute-start | bytes 1486856 | tf_op jit(solution)/shard_map/ppermute | solution.py:31
  258.2 9.0 %copy-start.3 = (f32[176,176]{1,0:T(8,128)S(1)}, f32[176,176]{1,0:T(8,128)}, u32[]{:S(2)}) copy-start(f32[176,176]{1,0:T(8,128)} %param.9) | copy-start | bytes 371716
  258.7 53.5 %collective-permute-start.20 = (f32[2,176,704]{2,1,0:T(8,128)S(1)}, f32[2,176,704]{2,1,0:T(8,128)}, u32[]{:S(2)}, u32[]{:S(2)}) collective-permute-start(f32[2,176,704]{2,1,0:T(8,128)S(1)} %copy.26), channel_id=1, source_target_pairs={{0,64},{8,72},{16,80},{24,88},{32,96},{40,104},{48,112},{56,120},{... | collective-permute-start | bytes 2973704 | tf_op jit(solution)/shard_map/ppermute | solution.py:31
  267.2 50.7 %collective-permute-start.25 = (f32[176,176]{1,0:T(8,128)S(1)}, f32[176,176]{1,0:T(8,128)S(1)}, u32[]{:S(2)}, u32[]{:S(2)}) collective-permute-start(f32[176,176]{1,0:T(8,128)S(1)} %copy-done.3), channel_id=1, source_target_pairs={{0,1},{1,2},{2,3},{3,4},{4,5},{5,6},{6,7},{7,0},{8,9},{9,10},{10,1... | collective-permute-start | bytes 371720 | tf_op jit(solution)/shard_map/ppermute | solution.py:15
  317.7 205.1 %reduce-scatter.9.cloned.1.call-start = ((), (), s32[]{:S(2)}) async-start(), calls=%async_computation.5 | async-start | bytes 1622016 | tf_op jit(solution)/shard_map/reduce_scatter | solution.py:66
  317.9 15.6 %collective-permute-start.26 = (f32[176,176]{1,0:T(8,128)S(1)}, f32[176,176]{1,0:T(8,128)S(1)}, u32[]{:S(2)}, u32[]{:S(2)}) collective-permute-start(f32[176,176]{1,0:T(8,128)S(1)} %collective-permute-done.25), channel_id=1, source_target_pairs={{0,1},{1,2},{2,3},{3,4},{4,5},{5,6},{6,7},{7,0},{8,9},{9,10},{10,1... | collective-permute-start | bytes 371720 | tf_op jit(solution)/shard_map/ppermute | solution.py:15
  318.0 15.6 %collective-permute-start.29 = (f32[176,176]{1,0:T(8,128)S(1)}, f32[176,176]{1,0:T(8,128)S(1)}, u32[]{:S(2)}, u32[]{:S(2)}) collective-permute-start(f32[176,176]{1,0:T(8,128)S(1)} %copy-done.3), channel_id=1, source_target_pairs={{0,7},{1,0},{2,1},{3,2},{4,3},{5,4},{6,5},{7,6},{8,15},{9,8},{10,9... | collective-permute-start | bytes 371720 | tf_op jit(solution)/shard_map/ppermute | solution.py:18
  333.6 12.8 %copy-start.9 = (f32[176,176]{1,0:T(8,128)}, f32[176,176]{1,0:T(8,128)S(1)}, u32[]{:S(2)}) copy-start(f32[176,176]{1,0:T(8,128)S(1)} %collective-permute-done.26) | copy-start | bytes 371716
  333.6 6.1 collective-permute-start.27
  333.6 9.2 %copy-start.7 = (f32[176,176]{1,0:T(8,128)}, f32[176,176]{1,0:T(8,128)S(1)}, u32[]{:S(2)}) copy-start(f32[176,176]{1,0:T(8,128)S(1)} %collective-permute-done.29) | copy-start | bytes 371716
  333.6 6.1 collective-permute-start.30
  339.7 6.6 %collective-permute-start.28 = (f32[176,176]{1,0:T(8,128)S(1)}, f32[176,176]{1,0:T(8,128)S(1)}, u32[]{:S(2)}, u32[]{:S(2)}) collective-permute-start(f32[176,176]{1,0:T(8,128)S(1)} %collective-permute-done.27), channel_id=1, source_target_pairs={{0,1},{1,2},{2,3},{3,4},{4,5},{5,6},{6,7},{7,0},{8,9},{9,10},{10,1... | collective-permute-start | bytes 371720 | tf_op jit(solution)/shard_map/ppermute | solution.py:15
  339.7 37.9 %collective-permute-start.31 = (f32[176,176]{1,0:T(8,128)}, f32[176,176]{1,0:T(8,128)}, u32[]{:S(2)}, u32[]{:S(2)}) collective-permute-start(f32[176,176]{1,0:T(8,128)} %collective-permute-done.30), channel_id=1, source_target_pairs={{0,7},{1,0},{2,1},{3,2},{4,3},{5,4},{6,5},{7,6},{8,15},{9,8},{10,9... | collective-permute-start | bytes 371720 | tf_op jit(solution)/shard_map/ppermute | solution.py:18
  364.9 20.3 %copy-start.14 = (f32[176,176]{1,0:T(8,128)S(1)}, f32[176,176]{1,0:T(8,128)}, u32[]{:S(2)}) copy-start(f32[176,176]{1,0:T(8,128)} %copy-done.13) | copy-start | bytes 371716
  364.9 20.3 %copy-start.12 = (f32[176,176]{1,0:T(8,128)S(1)}, f32[176,176]{1,0:T(8,128)}, u32[]{:S(2)}) copy-start(f32[176,176]{1,0:T(8,128)} %copy-done.11) | copy-start | bytes 371716
  364.9 20.3 %copy-start.10 = (f32[176,176]{1,0:T(8,128)S(1)}, f32[176,176]{1,0:T(8,128)}, u32[]{:S(2)}) copy-start(f32[176,176]{1,0:T(8,128)} %copy-done.9) | copy-start | bytes 371716
  364.9 6.8 %collective-permute-start.21 = (f32[176,88]{1,0:T(8,128)}, f32[176,88]{1,0:T(8,128)S(1)}, u32[]{:S(2)}, u32[]{:S(2)}) collective-permute-start(f32[176,88]{1,0:T(8,128)} %reduce-scatter.7.cloned.1.call-done), channel_id=1, source_target_pairs={{0,8},{8,0},{16,24},{24,16},{32,40},{40,32},{48,56},{56,48},{64,72... | collective-permute-start | bytes 185864 | tf_op jit(solution)/shard_map/ppermute | solution.py:31
  372.8 8.9 %collective-permute-start.22 = (f32[176,176]{1,0:T(8,128)S(1)}, f32[176,176]{1,0:T(8,128)S(1)}, u32[]{:S(2)}, u32[]{:S(2)}) collective-permute-start(f32[176,176]{1,0:T(8,128)S(1)} %maximum_select_fusion.27), channel_id=1, source_target_pairs={{0,16},{8,24},{16,0},{24,8},{32,48},{40,56},{48,32},{56,40},{64,80... | collective-permute-start | bytes 371720 | tf_op jit(solution)/shard_map/ppermute | solution.py:31
  377.6 18.7 %copy-start.8 = (f32[176,176]{1,0:T(8,128)S(1)}, f32[176,176]{1,0:T(8,128)}, u32[]{:S(2)}) copy-start(f32[176,176]{1,0:T(8,128)} %copy-done.7) | copy-start | bytes 371716
  381.9 9.9 %collective-permute-start.23 = (f32[176,352]{1,0:T(8,128)S(1)}, f32[176,352]{1,0:T(8,128)S(1)}, u32[]{:S(2)}, u32[]{:S(2)}) collective-permute-start(f32[176,352]{1,0:T(8,128)S(1)} %maximum_select_fusion.23), channel_id=1, source_target_pairs={{0,32},{8,40},{16,48},{24,56},{32,0},{40,8},{48,16},{56,24},{64,96... | collective-permute-start | bytes 743432 | tf_op jit(solution)/shard_map/ppermute | solution.py:31
  392.1 20.8 %collective-permute-start.24 = (f32[176,704]{1,0:T(8,128)S(1)}, f32[176,704]{1,0:T(8,128)S(1)}, u32[]{:S(2)}, u32[]{:S(2)}) collective-permute-start(f32[176,704]{1,0:T(8,128)S(1)} %maximum_select_fusion.17), channel_id=1, source_target_pairs={{0,64},{8,72},{16,80},{24,88},{32,96},{40,104},{48,112},{56,120},{... | collective-permute-start | bytes 1486856 | tf_op jit(solution)/shard_map/ppermute | solution.py:31
  396.4 17.8 %copy-start.4 = (f32[176,176]{1,0:T(8,128)S(1)}, f32[176,176]{1,0:T(8,128)}, u32[]{:S(2)}) copy-start(f32[176,176]{1,0:T(8,128)} %param.12) | copy-start | bytes 371716
  414.2 25.9 %copy-start.5 = (f32[176,176]{1,0:T(8,128)}, f32[176,176]{1,0:T(8,128)S(1)}, u32[]{:S(2)}) copy-start(f32[176,176]{1,0:T(8,128)S(1)} %fusion.8) | copy-start | bytes 371716
  414.2 10.3 %collective-permute-start.32 = (f32[2,176,176]{2,1,0:T(8,128)S(1)}, f32[2,176,176]{2,1,0:T(8,128)S(1)}, u32[]{:S(2)}, u32[]{:S(2)}) collective-permute-start(f32[2,176,176]{2,1,0:T(8,128)S(1)} %pad_maximum_fusion.1), channel_id=1, source_target_pairs={{0,8},{8,0},{16,24},{24,16},{32,40},{40,32},{48,56},{56,48},{64,72... | collective-permute-start | bytes 743432 | tf_op jit(solution)/shard_map/ppermute | solution.py:31
  424.8 14.8 %collective-permute-start.33 = (f32[2,176,352]{2,1,0:T(8,128)S(1)}, f32[2,176,352]{2,1,0:T(8,128)S(1)}, u32[]{:S(2)}, u32[]{:S(2)}) collective-permute-start(f32[2,176,352]{2,1,0:T(8,128)S(1)} %maximum_select_fusion.18), channel_id=1, source_target_pairs={{0,16},{8,24},{16,0},{24,8},{32,48},{40,56},{48,32},{56,40},{64,80... | collective-permute-start | bytes 1486856 | tf_op jit(solution)/shard_map/ppermute | solution.py:31
  440.1 23.9 %collective-permute-start.34 = (f32[2,176,704]{2,1,0:T(8,128)S(1)}, f32[2,176,704]{2,1,0:T(8,128)S(1)}, u32[]{:S(2)}, u32[]{:S(2)}) collective-permute-start(f32[2,176,704]{2,1,0:T(8,128)S(1)} %maximum_select_fusion.4), channel_id=1, source_target_pairs={{0,32},{8,40},{16,48},{24,56},{32,0},{40,8},{48,16},{56,24},{64,96... | collective-permute-start | bytes 2973704 | tf_op jit(solution)/shard_map/ppermute | solution.py:31
  470.9 182.7 %reduce-scatter.11.cloned.1.call-start = ((), (), s32[]{:S(2)}) async-start(), calls=%async_computation.6 | async-start | bytes 2433024 | tf_op jit(solution)/shard_map/reduce_scatter | solution.py:66
  470.9 12.7 %collective-permute-start.38 = (f32[176,352]{1,0:T(8,128)S(1)}, f32[176,352]{1,0:T(8,128)S(1)}, u32[]{:S(2)}, u32[]{:S(2)}) collective-permute-start(f32[176,352]{1,0:T(8,128)S(1)} %copy-done), channel_id=1, source_target_pairs={{0,1},{1,2},{2,3},{3,4},{4,5},{5,6},{6,7},{7,0},{8,9},{9,10},{10,1... | collective-permute-start | bytes 743432 | tf_op jit(solution)/shard_map/ppermute | solution.py:15
  483.7 7.1 %collective-permute-start.39 = (f32[176,352]{1,0:T(8,128)S(1)}, f32[176,352]{1,0:T(8,128)S(1)}, u32[]{:S(2)}, u32[]{:S(2)}) collective-permute-start(f32[176,352]{1,0:T(8,128)S(1)} %collective-permute-done.38), channel_id=1, source_target_pairs={{0,1},{1,2},{2,3},{3,4},{4,5},{5,6},{6,7},{7,0},{8,9},{9,10},{10,1... | collective-permute-start | bytes 743432 | tf_op jit(solution)/shard_map/ppermute | solution.py:15
  483.7 7.1 %collective-permute-start.42 = (f32[176,352]{1,0:T(8,128)S(1)}, f32[176,352]{1,0:T(8,128)S(1)}, u32[]{:S(2)}, u32[]{:S(2)}) collective-permute-start(f32[176,352]{1,0:T(8,128)S(1)} %copy-done), channel_id=1, source_target_pairs={{0,7},{1,0},{2,1},{3,2},{4,3},{5,4},{6,5},{7,6},{8,15},{9,8},{10,9... | collective-permute-start | bytes 743432 | tf_op jit(solution)/shard_map/ppermute | solution.py:18
  490.8 7.1 %collective-permute-start.40 = (f32[176,352]{1,0:T(8,128)S(1)}, f32[176,352]{1,0:T(8,128)S(1)}, u32[]{:S(2)}, u32[]{:S(2)}) collective-permute-start(f32[176,352]{1,0:T(8,128)S(1)} %collective-permute-done.39), channel_id=1, source_target_pairs={{0,1},{1,2},{2,3},{3,4},{4,5},{5,6},{6,7},{7,0},{8,9},{9,10},{10,1... | collective-permute-start | bytes 743432 | tf_op jit(solution)/shard_map/ppermute | solution.py:15
  490.8 7.1 %collective-permute-start.43 = (f32[176,352]{1,0:T(8,128)S(1)}, f32[176,352]{1,0:T(8,128)S(1)}, u32[]{:S(2)}, u32[]{:S(2)}) collective-permute-start(f32[176,352]{1,0:T(8,128)S(1)} %collective-permute-done.42), channel_id=1, source_target_pairs={{0,7},{1,0},{2,1},{3,2},{4,3},{5,4},{6,5},{7,6},{8,15},{9,8},{10,9... | collective-permute-start | bytes 743432 | tf_op jit(solution)/shard_map/ppermute | solution.py:18
  497.9 8.3 %collective-permute-start.41 = (f32[176,352]{1,0:T(8,128)S(1)}, f32[176,352]{1,0:T(8,128)S(1)}, u32[]{:S(2)}, u32[]{:S(2)}) collective-permute-start(f32[176,352]{1,0:T(8,128)S(1)} %collective-permute-done.40), channel_id=1, source_target_pairs={{0,1},{1,2},{2,3},{3,4},{4,5},{5,6},{6,7},{7,0},{8,9},{9,10},{10,1... | collective-permute-start | bytes 743432 | tf_op jit(solution)/shard_map/ppermute | solution.py:15
  497.9 28.0 %collective-permute-start.44 = (f32[176,352]{1,0:T(8,128)S(1)}, f32[176,352]{1,0:T(8,128)S(1)}, u32[]{:S(2)}, u32[]{:S(2)}) collective-permute-start(f32[176,352]{1,0:T(8,128)S(1)} %collective-permute-done.43), channel_id=1, source_target_pairs={{0,7},{1,0},{2,1},{3,2},{4,3},{5,4},{6,5},{7,6},{8,15},{9,8},{10,9... | collective-permute-start | bytes 743432 | tf_op jit(solution)/shard_map/ppermute | solution.py:18
  522.8 7.6 %collective-permute-start.35 = (f32[176,176]{1,0:T(8,128)}, f32[176,176]{1,0:T(8,128)S(1)}, u32[]{:S(2)}, u32[]{:S(2)}) collective-permute-start(f32[176,176]{1,0:T(8,128)} %reduce-scatter.9.cloned.1.call-done), channel_id=1, source_target_pairs={{0,8},{8,0},{16,24},{24,16},{32,40},{40,32},{48,56},{56,48},{64,72... | collective-permute-start | bytes 371720 | tf_op jit(solution)/shard_map/ppermute | solution.py:31
  531.6 9.9 %collective-permute-start.36 = (f32[176,352]{1,0:T(8,128)S(1)}, f32[176,352]{1,0:T(8,128)S(1)}, u32[]{:S(2)}, u32[]{:S(2)}) collective-permute-start(f32[176,352]{1,0:T(8,128)S(1)} %maximum_select_fusion.24), channel_id=1, source_target_pairs={{0,16},{8,24},{16,0},{24,8},{32,48},{40,56},{48,32},{56,40},{64,80... | collective-permute-start | bytes 743432 | tf_op jit(solution)/shard_map/ppermute | solution.py:31
  541.7 11.3 %collective-permute-start.37 = (f32[176,704]{1,0:T(8,128)S(1)}, f32[176,704]{1,0:T(8,128)S(1)}, u32[]{:S(2)}, u32[]{:S(2)}) collective-permute-start(f32[176,704]{1,0:T(8,128)S(1)} %maximum_select_fusion.19), channel_id=1, source_target_pairs={{0,32},{8,40},{16,48},{24,56},{32,0},{40,8},{48,16},{56,24},{64,96... | collective-permute-start | bytes 1486856 | tf_op jit(solution)/shard_map/ppermute | solution.py:31
  556.9 36.8 %copy-start.2 = (f32[176,352]{1,0:T(8,128)}, f32[176,352]{1,0:T(8,128)S(1)}, u32[]{:S(2)}) copy-start(f32[176,352]{1,0:T(8,128)S(1)} %fusion.5) | copy-start | bytes 743428
  556.9 12.7 %collective-permute-start.45 = (f32[2,176,352]{2,1,0:T(8,128)S(1)}, f32[2,176,352]{2,1,0:T(8,128)S(1)}, u32[]{:S(2)}, u32[]{:S(2)}) collective-permute-start(f32[2,176,352]{2,1,0:T(8,128)S(1)} %pad_maximum_fusion), channel_id=1, source_target_pairs={{0,8},{8,0},{16,24},{24,16},{32,40},{40,32},{48,56},{56,48},{64,72... | collective-permute-start | bytes 1486856 | tf_op jit(solution)/shard_map/ppermute | solution.py:31
  570.1 23.0 %collective-permute-start.46 = (f32[2,176,704]{2,1,0:T(8,128)S(1)}, f32[2,176,704]{2,1,0:T(8,128)S(1)}, u32[]{:S(2)}, u32[]{:S(2)}) collective-permute-start(f32[2,176,704]{2,1,0:T(8,128)S(1)} %maximum_select_fusion.5), channel_id=1, source_target_pairs={{0,16},{8,24},{16,0},{24,8},{32,48},{40,56},{48,32},{56,40},{64,80... | collective-permute-start | bytes 2973704 | tf_op jit(solution)/shard_map/ppermute | solution.py:31
  (5 other events, 20.7 us)
Sparse Core Ops, SparseCore 0:
  102.8 40.1 reduce-scatter.12
  317.8 47.0 reduce-scatter.6
  471.0 51.7 reduce-scatter.8
  600.4 53.1 reduce-scatter.10
